TPU v7x, 256 devices: a whole 4x4x8 slice. The times are simulated.
256 devices in a mesh: tm: 8 (over z_lo, core), height: 32 (over x, y, z_hi).
Axes of the slice: x: 4, y: 4, z: 8 (z_hi: 2, z_lo: 4; z = z_hi * 4 + z_lo), core: 2. Of those that a mesh axis runs over, the one named last changes fastest.
Arguments:
- clean_latents: bfloat16 [32, 128, 16, 3072], P('tm', 'height'), may hold values from -6 to 6
- gaussian_noise: bfloat16 [32, 128, 16, 3072], P('tm', 'height'), may hold values from -6 to 6
- text_states: bfloat16 [256, 3072], replicated, may hold values from -6 to 6
- queries: bfloat16 [32, 128, 16, 1536], P('tm', 'height'), may hold values from -40 to 40
- key_states: bfloat16 [32, 128, 16, 1536], P('tm', 'height'), may hold values from -8 to 8
- cotangent: bfloat16 [32, 128, 16, 1536], P('tm', 'height'), may hold values from -240 to 240
- text_keys: bfloat16 [256, 1536], replicated, may hold values from -6 to 6
- window_radii: int32 [12, 3], replicated, may hold values from 0 to 1
- timestep: int32 [1], replicated, may hold values from 200 to 799
- sketch_seed: int32 [1], replicated, may hold values from 0 to 65535
- down_image: bfloat16 [3072, 16], replicated, may hold values from -0.109375 to 0.109375
- up_image: bfloat16 [16, 1536], replicated, may hold values from -1.5 to 1.5
- down_text: bfloat16 [3072, 16], replicated, may hold values from -0.109375 to 0.109375
- up_text: bfloat16 [16, 1536], replicated, may hold values from -1.5 to 1.5
Outputs:
- value_grad: bfloat16 [32, 128, 16, 1536], P('tm', 'height')
- grad_sketch: float32 [16384], replicated
All inputs are finite; a program needn't handle non-finite values.
Results may differ from a plain program's by a relative error of at most 0.0075.
Values may be sent and summed in bfloat16 or wider, within the bound.
A program may use at most 128 MiB of HBM per device.

v0:
```python
import jax
import jax.numpy as jnp
from jax import lax
from jax.sharding import PartitionSpec as P

SKETCH = 16384
TW = 8


def padded_2(block, sides, width):
    for axis, dim in sides:
        count = lax.axis_size(axis)
        forward = [(i, i + 1) for i in range(count - 1)]
        backward = [(target, source) for source, target in forward]
        low = lax.ppermute(
            lax.slice_in_dim(block, block.shape[dim] - width, None, axis=dim), axis, forward
        )
        high = lax.ppermute(lax.slice_in_dim(block, 0, width, axis=dim), axis, backward)
        block = jnp.concatenate([low, block, high], axis=dim)
    return block


def shifted(array, axis, by):
    size = lax.axis_size(axis)
    pairs = [(i, i + by) for i in range(size) if 0 <= i + by < size]
    return lax.ppermute(array, axis, pairs)


def tile_rows(block, width):
    frame_count, row_count, col_count = (block.shape[0], block.shape[1], block.shape[2])
    rest = block.shape[3:]
    col_tiles = col_count // width
    shaped = block.reshape((frame_count, row_count, col_tiles, width) + rest)
    order = (2, 0, 1, 3) + tuple(range(4, 4 + len(rest)))
    return jnp.transpose(shaped, order).reshape((col_tiles, frame_count * row_count * width) + rest)


def region_rows(padded, width):
    col_count = padded.shape[2] - 2 * width
    views = [
        tile_rows(padded[:, :, shift_col * width : shift_col * width + col_count], width)
        for shift_col in range(3)
    ]
    return jnp.concatenate(views, axis=1)


def window_mask(
    radius, frame_tile, row_tile, frame_tiles, row_tiles, col_tiles, frame_count, row_count, width
):
    region = 27 * frame_count * row_count * width
    position = jnp.arange(region, dtype=jnp.int32)
    col_step = position // (9 * frame_count * row_count * width) - 1
    frame_step = position // (3 * row_count * width) % (3 * frame_count) // frame_count - 1
    row_step = position // width % (3 * row_count) // row_count - 1
    inside = (
        (jnp.abs(frame_step) <= radius[0])
        & (jnp.abs(row_step) <= radius[1])
        & (jnp.abs(col_step) <= radius[2])
    )
    inside = inside & (frame_tile + frame_step >= 0) & (frame_tile + frame_step < frame_tiles)
    inside = inside & (row_tile + row_step >= 0) & (row_tile + row_step < row_tiles)
    col_index = jnp.arange(col_tiles, dtype=jnp.int32)[:, None]
    return (
        inside[None, :]
        & (col_index + col_step[None, :] >= 0)
        & (col_index + col_step[None, :] < col_tiles)
    )


def forward_head(query_head, key_region, text_head, cot_head, allowed, score_scale):
    image_scores = (
        jnp.einsum("cqd,cld->cql", query_head, key_region, preferred_element_type=jnp.float32)
        * score_scale
    )
    image_scores = jnp.where(allowed[:, None, :], image_scores, -jnp.inf)
    text_scores = (
        jnp.einsum("cqd,td->cqt", query_head, text_head, preferred_element_type=jnp.float32)
        * score_scale
    )
    row_max = jnp.maximum(jnp.max(image_scores, axis=-1), jnp.max(text_scores, axis=-1))
    total = jnp.sum(jnp.exp(image_scores - row_max[..., None]), axis=-1) + jnp.sum(
        jnp.exp(text_scores - row_max[..., None]), axis=-1
    )
    log_total = row_max + jnp.log(total)
    text_probs = jnp.exp(text_scores - log_total[..., None]).astype(jnp.bfloat16)
    text_part = jnp.einsum("cqt,cqd->td", text_probs, cot_head, preferred_element_type=jnp.float32)
    return (image_scores, log_total, text_part)


def place_back(spread, frame_count, row_count, width):
    col_tiles, head_width = (spread.shape[0], spread.shape[2])
    shaped = spread.reshape(col_tiles, 3, 3 * frame_count, 3 * row_count, width, head_width)
    placed = jnp.zeros((3 * frame_count, 3 * row_count, col_tiles, width, head_width), jnp.float32)
    for shift_col in range(3):
        moved = jnp.transpose(shaped[:, shift_col], (1, 2, 0, 3, 4))
        moved = jnp.pad(moved, ((0, 0), (0, 0), (1, 1), (0, 0), (0, 0)))
        placed = placed + moved[:, :, 2 - shift_col : 2 - shift_col + col_tiles]
    return placed.reshape(3 * frame_count, 3 * row_count, col_tiles * width, head_width)


def sketch_signs(seed_value, rows, width):
    row_part = jnp.arange(rows, dtype=jnp.int32)[:, None] * width
    position = row_part + jnp.arange(width, dtype=jnp.int32)[None, :]
    mixed_bits = position * 1103515245 + seed_value * 12345 + 1013904223
    mixed_bits = mixed_bits ^ mixed_bits >> 16
    mixed_bits = mixed_bits * 73244475
    mixed_bits = mixed_bits ^ mixed_bits >> 16
    return (1 - 2 * (mixed_bits >> 7 & 1)).astype(jnp.float32)


def count_sketch(pieces, seed_value, width, sketch_scale):
    flat = jnp.concatenate([piece.reshape(-1) for piece in pieces]).reshape(-1, width)
    signed = flat * sketch_signs(seed_value, flat.shape[0], width)
    return jnp.sum(signed, axis=0) * sketch_scale


def text_grads(text_hidden, text_value, text_states, up_text):
    highest = lax.Precision.HIGHEST
    text_up_grad = jnp.dot(text_hidden.T, text_value, precision=highest)
    text_back = jnp.dot(text_value, up_text.astype(jnp.float32).T, precision=highest)
    text_down_grad = jnp.dot(text_states.astype(jnp.float32).T, text_back, precision=highest)
    return (text_down_grad, text_up_grad)


def per_device(
    clean_latents,
    gaussian_noise,
    text_states,
    queries,
    key_states,
    cotangent,
    text_keys,
    window_radii,
    timestep,
    sketch_seed,
    down_image,
    up_image,
    down_text,
    up_text,
):
    frame_count, row_count, col_count, value_width = queries.shape
    head_count = window_radii.shape[0]
    head_width = value_width // head_count
    col_tiles = col_count // TW
    score_scale = head_width ** (-0.5)
    frame_tile = lax.axis_index("tm")
    row_tile = lax.axis_index("height")
    frame_tiles = lax.axis_size("tm")
    row_tiles = lax.axis_size("height")
    pad_spec = ((0, 0), (0, 0), (TW, TW), (0, 0))
    key_pad = jnp.pad(padded_2(key_states, (("tm", 0), ("height", 1)), frame_count), pad_spec)
    own_q = tile_rows(queries, TW)
    own_c = tile_rows(cotangent, TW)
    head_ids = jnp.arange(head_count, dtype=jnp.int32)

    def head_mask(head_index):
        return window_mask(
            window_radii[head_index],
            frame_tile,
            row_tile,
            frame_tiles,
            row_tiles,
            col_tiles,
            frame_count,
            row_count,
            TW,
        )

    def forward(head_index):
        offset = head_index * head_width
        allowed = head_mask(head_index)
        query_head = lax.dynamic_slice_in_dim(own_q, offset, head_width, 2)
        cot_head = lax.dynamic_slice_in_dim(own_c, offset, head_width, 2)
        key_region = region_rows(lax.dynamic_slice_in_dim(key_pad, offset, head_width, 3), TW)
        text_head = lax.dynamic_slice_in_dim(text_keys, offset, head_width, 1)
        image_scores, log_total, text_part = forward_head(
            query_head, key_region, text_head, cot_head, allowed, score_scale
        )
        image_probs = jnp.exp(image_scores - log_total[..., None]).astype(jnp.bfloat16)
        spread = jnp.einsum(
            "cql,cqd->cld", image_probs, cot_head, preferred_element_type=jnp.float32
        )
        return (text_part, place_back(spread, frame_count, row_count, TW))

    text_part, head_out = lax.map(forward, head_ids)
    text_value = jnp.transpose(text_part, (1, 0, 2)).reshape(-1, value_width)
    middle = head_out[:, :, row_count : 2 * row_count]
    for direction, border in (
        (-1, head_out[:, :, :row_count]),
        (1, head_out[:, :, 2 * row_count :]),
    ):
        middle = middle + shifted(border.astype(jnp.bfloat16), "height", direction).astype(
            border.dtype
        )
    own_part = middle[:, frame_count : 2 * frame_count]
    for direction, border in ((-1, middle[:, :frame_count]), (1, middle[:, 2 * frame_count :])):
        own_part = own_part + shifted(border.astype(jnp.bfloat16), "tm", direction).astype(
            border.dtype
        )
    value_f32 = jnp.transpose(own_part, (1, 2, 3, 0, 4)).reshape(
        frame_count, row_count, col_count, value_width
    )
    value_grad = value_f32.astype(jnp.bfloat16)
    noise_level = timestep[0].astype(jnp.float32) / 1000.0
    mixed = (
        (1.0 - noise_level) * clean_latents.astype(jnp.float32)
        + noise_level * gaussian_noise.astype(jnp.float32)
    ).astype(jnp.bfloat16)
    mixed = mixed.reshape(-1, mixed.shape[3])
    flat_value = value_grad.reshape(-1, value_width)
    hidden = jnp.dot(mixed, down_image, preferred_element_type=jnp.float32).astype(jnp.bfloat16)
    grad_up = lax.dot_general(
        hidden, flat_value, (((0,), (0,)), ((), ())), preferred_element_type=jnp.float32
    )
    backward_low = lax.dot_general(
        flat_value, up_image, (((1,), (1,)), ((), ())), preferred_element_type=jnp.float32
    ).astype(jnp.bfloat16)
    grad_down = lax.dot_general(
        mixed, backward_low, (((0,), (0,)), ((), ())), preferred_element_type=jnp.float32
    )
    text_hidden = jnp.dot(text_states, down_text, preferred_element_type=jnp.float32)
    token_total = frame_count * row_count * col_count * frame_tiles * row_tiles
    param_total = 2 * grad_down.size + 2 * grad_up.size
    sketch_scale = (token_total * (param_total // SKETCH)) ** (-0.5)
    text_down_grad, text_up_grad = text_grads(text_hidden, text_value, text_states, up_text)
    local_sketch = count_sketch(
        (grad_down, grad_up, text_down_grad, text_up_grad), sketch_seed[0], SKETCH, sketch_scale
    )
    grad_sketch = lax.psum(local_sketch, ("tm", "height"))
    return (value_grad, grad_sketch)


def solution(mesh):
    return jax.shard_map(
        per_device,
        mesh=mesh,
        in_specs=(
            P("tm", "height", None, None),
            P("tm", "height", None, None),
            P(),
            P("tm", "height", None, None),
            P("tm", "height", None, None),
            P("tm", "height", None, None),
            P(),
            P(),
            P(),
            P(),
            P(),
            P(),
            P(),
            P(),
        ),
        out_specs=(P("tm", "height", None, None), P()),
        check_vma=False,
    )
```

profile of v0, /device:TPU:1, one launch (start us, length us, event | category | flops | bytes accessed | tf_op | source)
XLA Modules:
  0.0 920.2 jit_solution(15900157499959258757)
XLA Ops:
  7.2 5.1 collective-permute-start
  14.2 7.3 collective-permute-done
  22.5 2.1 constant_dynamic-update-slice_fusion.1
  28.1 12.5 %collective-permute-start.2 = (bf16[12,4,16,1536]{3,2,1,0:T(8,128)(2,1)}, bf16[12,4,16,1536]{3,2,1,0:T(8,128)(2,1)}, u32[]{:S(2)}, u32[]{:S(2)}) collective-permute-start(bf16[12,4,16,1536]{3,2,1,0:T(8,128)(2,1)} %constant_dynamic-update-slice_fusion), channel_id=1, source_target_pairs={{0,1},{1,2},{2,3},{3,4},{4,5},{5,6},{6,7},{7,8},{8,9},{9,10},{10,1... | collective-permute-start | bytes 7077896 | tf_op jit(solution)/shard_map/ppermute | solution.py:15
  40.7 2.1 copy.51
  42.8 97.1 %collective-permute-done.3 = bf16[12,4,16,1536]{3,2,1,0:T(8,128)(2,1)} collective-permute-done((bf16[12,4,16,1536]{3,2,1,0:T(8,128)(2,1)}, bf16[12,4,16,1536]{3,2,1,0:T(8,128)(2,1)}, u32[]{:S(2)}, u32[]{:S(2)}) %collective-permute-start.3) | collective-permute-done | bytes 2359328 | tf_op jit(solution)/shard_map/ppermute | solution.py:18
  139.9 9.7 %fusion.52 = bf16[12,12,32,1536]{3,2,1,0:T(8,128)(2,1)} fusion(bf16[12,4,16,1536]{3,2,1,0:T(8,128)(2,1)} %collective-permute-done.3, bf16[12,4,16,1536]{3,2,1,0:T(8,128)(2,1)} %constant_dynamic-update-slice_fusion, bf16[12,4,16,1536]{3,2,1,0:T(8,128)(2,1)} %collective-permute-done.2), kind=kLoop, calls=%fused_computation.99 | loop fusion | flops 84934656 | bytes 21233664 | tf_op jit(solution)/shard_map/concatenate | solution.py:19
  149.6 213.1 %while.15 = (s32[]{:T(128)}, f32[12,256,128]{1,2,0:T(8,128)}, f32[12,12,12,16,128]{4,3,2,1,0:T(8,128)}, s32[12]{0:T(128)S(1)}, bf16[2,128,1536]{2,1,0:T(8,128)(2...) while((s32[]{:T(128)}, f32[12,256,128]{1,2,0:T(8,128)}, ...), condition=%wide.region_5.6_spmd, body=%wide.region_0.5_spmd.sunk | while | flops 499376128 | bytes 40042176 | solution.py:185
  258.5 2.0 dynamic-slice_bitcast_fusion.4
  362.7 9.7 %convert.8 = bf16[12,12,12,16,128]{4,3,2,1,0:T(8,128)(2,1)} convert(f32[12,12,12,16,128]{4,3,2,1,0:T(8,128)} %get-tuple-element.191) | non-fusion elementwise | flops 3538944 | bytes 21233664 | tf_op jit(solution)/shard_map/convert.3
  372.4 6.3 fusion.75
  378.7 42.7 %collective-permute-start.5 = (bf16[12,12,4,16,128]{4,3,2,1,0:T(8,128)(2,1)}, bf16[12,12,4,16,128]{4,3,2,1,0:T(8,128)(2,1)}, u32[]{:S(2)}, u32[]{:S(2)}) collective-permute-start(bf16[12,12,4,16,128]{4,3,2,1,0:T(8,128)(2,1)} %get-tuple-element.230), channel_id=1, source_target_pairs={{0,1},{1,2},{2,3},{3,4},{4,5},{5,6},{6,7},{7,8},{8,9},{9,10},{10,1... | collective-permute-start | bytes 7077896 | tf_op jit(solution)/shard_map/ppermute | solution.py:26
  424.5 2.6 add_convert_fusion
  427.1 34.4 %collective-permute-done.5 = bf16[12,12,4,16,128]{4,3,2,1,0:T(8,128)(2,1)} collective-permute-done((bf16[12,12,4,16,128]{4,3,2,1,0:T(8,128)(2,1)}, bf16[12,12,4,16,128]{4,3,2,1,0:T(8,128)(2,1)}, u32[]{:S(2)}, u32[]{:S(2)}) %collective-permute-start.5) | collective-permute-done | bytes 2359328 | tf_op jit(solution)/shard_map/ppermute | solution.py:26
  461.5 108.8 %collective-permute-done.4 = bf16[12,12,4,16,128]{4,3,2,1,0:T(8,128)(2,1)} collective-permute-done((bf16[12,12,4,16,128]{4,3,2,1,0:T(8,128)(2,1)}, bf16[12,12,4,16,128]{4,3,2,1,0:T(8,128)(2,1)}, u32[]{:S(2)}, u32[]{:S(2)}) %collective-permute-start.4) | collective-permute-done | bytes 2359328 | tf_op jit(solution)/shard_map/ppermute | solution.py:26
  570.3 7.4 fusion.71
  579.3 61.7 %collective-permute-start.7 = (bf16[12,4,4,16,128]{4,3,2,1,0:T(8,128)(2,1)}, bf16[12,4,4,16,128]{4,3,2,1,0:T(8,128)(2,1)}, u32[]{:S(2)}, u32[]{:S(2)}) collective-permute-start(bf16[12,4,4,16,128]{4,3,2,1,0:T(8,128)(2,1)} %get-tuple-element.232), channel_id=1, source_target_pairs={{0,32},{32,64},{64,96},{96,128},{128,160},{160,192},{192,224},{1,3... | collective-permute-start | bytes 2359304 | tf_op jit(solution)/shard_map/ppermute | solution.py:26
  641.1 2.1 collective-permute-start.6
  644.6 2.0 fusion.77
  650.9 3.8 collective-permute-done.6
  654.7 2.2 fusion.54
  659.3 2.2 fusion.55
  662.2 3.7 fusion.56
  672.2 239.7 %all-reduce.5.cloned.1.call-done = f32[16384]{0:T(1024)} async-done(((f32[16384]{0:T(1024)}), f32[16384]{0:T(1024)}) %all-reduce.5.cloned.1.call-update) | async-done | bytes 65552 | tf_op jit(solution)/shard_map/psum | solution.py:229
  (336 shorter events, 206.4 us)
Async XLA Ops:
  7.2 416.8 %copy-start = (bf16[256,3072]{1,0:T(8,128)(2,1)S(1)}, bf16[256,3072]{1,0:T(8,128)(2,1)}, u32[]{:S(2)}) copy-start(bf16[256,3072]{1,0:T(8,128)(2,1)} %param.18) | copy-start | bytes 4718596
  7.2 33.5 %copy-start.6 = (bf16[4,4,16,1536]{3,2,1,0:T(8,128)(2,1)S(1)}, bf16[4,4,16,1536]{3,2,1,0:T(8,128)(2,1)}, u32[]{:S(2)}) copy-start(bf16[4,4,16,1536]{3,2,1,0:T(8,128)(2,1)} %param.19) | copy-start | bytes 2359300
  7.2 904.7 %all-reduce.5.cloned.1.call-start = ((), (), s32[]{:S(2)}) async-start(), calls=%async_computation | async-start | bytes 131072 | tf_op jit(solution)/shard_map/psum | solution.py:229
  7.2 14.3 %collective-permute-start = (bf16[4,4,16,1536]{3,2,1,0:T(8,128)(2,1)}, bf16[4,4,16,1536]{3,2,1,0:T(8,128)(2,1)S(1)}, u32[]{:S(2)}, u32[]{:S(2)}) collective-permute-start(bf16[4,4,16,1536]{3,2,1,0:T(8,128)(2,1)} %param.20), channel_id=1, source_target_pairs={{0,32},{32,64},{64,96},{96,128},{128,160},{160,192},{192,224},{1,3... | collective-permute-start | bytes 2359304 | tf_op jit(solution)/shard_map/ppermute | solution.py:15
  12.3 13.5 %collective-permute-start.1 = (bf16[4,4,16,1536]{3,2,1,0:T(8,128)(2,1)}, bf16[4,4,16,1536]{3,2,1,0:T(8,128)(2,1)S(1)}, u32[]{:S(2)}, u32[]{:S(2)}) collective-permute-start(bf16[4,4,16,1536]{3,2,1,0:T(8,128)(2,1)} %param.20), channel_id=1, source_target_pairs={{32,0},{64,32},{96,64},{128,96},{160,128},{192,160},{224,192},{33,... | collective-permute-start | bytes 2359304 | tf_op jit(solution)/shard_map/ppermute | solution.py:18
  26.8 113.1 %collective-permute-start.3 = (bf16[12,4,16,1536]{3,2,1,0:T(8,128)(2,1)}, bf16[12,4,16,1536]{3,2,1,0:T(8,128)(2,1)}, u32[]{:S(2)}, u32[]{:S(2)}) collective-permute-start(bf16[12,4,16,1536]{3,2,1,0:T(8,128)(2,1)} %constant_dynamic-update-slice_fusion), channel_id=1, source_target_pairs={{1,0},{2,1},{3,2},{4,3},{5,4},{6,5},{7,6},{8,7},{9,8},{10,9},{11,1... | collective-permute-start | bytes 7077896 | tf_op jit(solution)/shard_map/ppermute | solution.py:18
  28.1 111.8 %collective-permute-start.2 = (bf16[12,4,16,1536]{3,2,1,0:T(8,128)(2,1)}, bf16[12,4,16,1536]{3,2,1,0:T(8,128)(2,1)}, u32[]{:S(2)}, u32[]{:S(2)}) collective-permute-start(bf16[12,4,16,1536]{3,2,1,0:T(8,128)(2,1)} %constant_dynamic-update-slice_fusion), channel_id=1, source_target_pairs={{0,1},{1,2},{2,3},{3,4},{4,5},{5,6},{6,7},{7,8},{8,9},{9,10},{10,1... | collective-permute-start | bytes 7077896 | tf_op jit(solution)/shard_map/ppermute | solution.py:15
  42.8 106.8 %copy-start.9 = (s32[12,3]{0,1:T(4,128)S(1)}, s32[12,3]{0,1:T(4,128)}, u32[]{:S(2)}) copy-start(s32[12,3]{0,1:T(4,128)} %param.23) | copy-start | bytes 436
  167.3 4.4 copy-start.4
  185.1 4.5 copy-start.4
  238.3 4.3 copy-start.4
  256.1 4.5 copy-start.4
  273.9 4.3 copy-start.4
  309.3 4.4 copy-start.4
  327.1 4.4 copy-start.4
  344.9 4.4 copy-start.4
  372.4 51.6 %copy-start.8 = (bf16[3072,16]{0,1:T(8,128)(2,1)S(1)}, bf16[3072,16]{0,1:T(8,128)(2,1)}, u32[]{:S(2)}) copy-start(bf16[3072,16]{0,1:T(8,128)(2,1)} %param.28) | copy-start | bytes 294916
  378.7 82.8 %collective-permute-start.5 = (bf16[12,12,4,16,128]{4,3,2,1,0:T(8,128)(2,1)}, bf16[12,12,4,16,128]{4,3,2,1,0:T(8,128)(2,1)}, u32[]{:S(2)}, u32[]{:S(2)}) collective-permute-start(bf16[12,12,4,16,128]{4,3,2,1,0:T(8,128)(2,1)} %get-tuple-element.230), channel_id=1, source_target_pairs={{0,1},{1,2},{2,3},{3,4},{4,5},{5,6},{6,7},{7,8},{8,9},{9,10},{10,1... | collective-permute-start | bytes 7077896 | tf_op jit(solution)/shard_map/ppermute | solution.py:26
  421.4 148.9 %collective-permute-start.4 = (bf16[12,12,4,16,128]{4,3,2,1,0:T(8,128)(2,1)}, bf16[12,12,4,16,128]{4,3,2,1,0:T(8,128)(2,1)}, u32[]{:S(2)}, u32[]{:S(2)}) collective-permute-start(bf16[12,12,4,16,128]{4,3,2,1,0:T(8,128)(2,1)} %get-tuple-element.229), channel_id=1, source_target_pairs={{1,0},{2,1},{3,2},{4,3},{5,4},{6,5},{7,6},{8,7},{9,8},{10,9},{11,1... | collective-permute-start | bytes 7077896 | tf_op jit(solution)/shard_map/ppermute | solution.py:26
  577.7 65.5 %copy-start.3 = (f32[12,256,128]{1,2,0:T(8,128)S(1)}, f32[12,256,128]{1,2,0:T(8,128)}, u32[]{:S(2)}) copy-start(f32[12,256,128]{1,2,0:T(8,128)} %get-tuple-element.192) | copy-start | bytes 4718596
  577.7 66.9 %copy-start.10 = (bf16[16,1536]{1,0:T(8,128)(2,1)S(1)}, bf16[16,1536]{1,0:T(8,128)(2,1)}, u32[]{:S(2)}) copy-start(bf16[16,1536]{1,0:T(8,128)(2,1)} %param.29) | copy-start | bytes 147460
  579.3 71.6 %collective-permute-start.7 = (bf16[12,4,4,16,128]{4,3,2,1,0:T(8,128)(2,1)}, bf16[12,4,4,16,128]{4,3,2,1,0:T(8,128)(2,1)}, u32[]{:S(2)}, u32[]{:S(2)}) collective-permute-start(bf16[12,4,4,16,128]{4,3,2,1,0:T(8,128)(2,1)} %get-tuple-element.232), channel_id=1, source_target_pairs={{0,32},{32,64},{64,96},{96,128},{128,160},{160,192},{192,224},{1,3... | collective-permute-start | bytes 2359304 | tf_op jit(solution)/shard_map/ppermute | solution.py:26
  641.1 13.6 %collective-permute-start.6 = (bf16[12,4,4,16,128]{4,3,2,1,0:T(8,128)(2,1)}, bf16[12,4,4,16,128]{4,3,2,1,0:T(8,128)(2,1)}, u32[]{:S(2)}, u32[]{:S(2)}) collective-permute-start(bf16[12,4,4,16,128]{4,3,2,1,0:T(8,128)(2,1)} %get-tuple-element.231), channel_id=1, source_target_pairs={{32,0},{64,32},{96,64},{128,96},{160,128},{192,160},{224,192},{33,... | collective-permute-start | bytes 2359304 | tf_op jit(solution)/shard_map/ppermute | solution.py:26
  662.2 5.5 copy-start.7
  (18 other events, 36.4 us)
Sparse Core Ops, SparseCore 0:
  671.3 240.5 all-reduce.4
where the time goes:
time: 925 us; the launch traced here: 920 us
  waiting for transfers between devices  492 us (53%)
  starting transfers between devices  129 us (14%)
  matrix products  89.3 us (10%)
  other arithmetic  82 us (9%)
  local copies, waits for them, and re-layouts  81.4 us (9%)
  loops' own time  31 us (3%)
  between operations  15.5 us (2%)
    psum x1, waiting for transfers between devices, per_device(): grad_sketch = lax.psum(local_sketch, ('tm', 'height'))  240 us
    ppermute x4, waiting for transfers between devices, shifted(): return lax.ppermute(array, axis, pairs)  147 us
    ppermute x4, starting transfers between devices, shifted(): return lax.ppermute(array, axis, pairs)  108 us
    ppermute x2, waiting for transfers between devices, padded_2(): lax.ppermute(lax.slice_in_dim(block, 0, width, axis=dim), axis, backward)  98.3 us
    reshape x50, local copies, waits for them, and re-layouts, tile_rows(): shaped = block.reshape((frame_count, row_count, col_tiles, width) + rest)  38.7 us
    another operation x1, loops' own time, per_device(): text_part, head_out = lax.map(forward, head_ids)  31 us
    and x12, other arithmetic, window_mask(): inside & (row_tile + row_step >= 0) & (row_tile + row_step < row_tiles)  23 us
    dot_general x12, matrix products, forward(): jnp.einsum('cql,cqd->cld', image_probs, cot_head, preferred_element_type=...  22.2 us
  transfers between devices with their start and end apart: 9, of which 7 were waited for; matrix products, arithmetic and copies ran while one was open for 2% of the time, Pallas kernels for 0%

commit v1 on v0

--- a/solution.py
+++ b/solution.py
@@ -226,7 +226,7 @@
     local_sketch = count_sketch(
         (grad_down, grad_up, text_down_grad, text_up_grad), sketch_seed[0], SKETCH, sketch_scale
     )
-    grad_sketch = lax.psum(local_sketch, ("tm", "height"))
+    grad_sketch = lax.psum(lax.psum(local_sketch, "tm"), "height")
     return (value_grad, grad_sketch)
 
 

time: 925 us -> 1150 us (1.24)
  the two profiles are of different devices: /device:TPU:1 before, /device:TPU:32 now
where the time goes in v1:
time: 1150 us
  waiting for transfers between devices  723 us (63%)
  starting transfers between devices  125 us (11%)
  matrix products  89.3 us (8%)
  other arithmetic  82 us (7%)
  local copies, waits for them, and re-layouts  81.4 us (7%)
  loops' own time  31 us (3%)
  between operations  15.5 us (1%)
    psum x2, waiting for transfers between devices, per_device(): grad_sketch = lax.psum(lax.psum(local_sketch, 'tm'), 'height')  470 us
    ppermute x4, waiting for transfers between devices, shifted(): return lax.ppermute(array, axis, pairs)  149 us
    ppermute x4, starting transfers between devices, shifted(): return lax.ppermute(array, axis, pairs)  107 us
    ppermute x2, waiting for transfers between devices, padded_2(): lax.ppermute(lax.slice_in_dim(block, 0, width, axis=dim), axis, backward)  96 us
    reshape x50, local copies, waits for them, and re-layouts, tile_rows(): shaped = block.reshape((frame_count, row_count, col_tiles, width) + rest)  38.7 us
    another operation x1, loops' own time, per_device(): text_part, head_out = lax.map(forward, head_ids)  31 us
    and x12, other arithmetic, window_mask(): inside & (row_tile + row_step >= 0) & (row_tile + row_step < row_tiles)  23 us
  transfers between devices with their start and end apart: 10, of which 8 were waited for; matrix products, arithmetic and copies ran while one was open for 1% of the time, Pallas kernels for 0%

profile of v1, /device:TPU:32, one launch (start us, length us, event | category | flops | bytes accessed | tf_op | source)
XLA Modules:
  0.0 1147.1 jit_solution(4695779078489295157)
XLA Ops:
  7.2 2.1 collective-permute-start
  9.3 3.6 collective-permute-start.1
  12.9 7.9 collective-permute-done
  21.9 2.1 constant_dynamic-update-slice_fusion.1
  26.2 11.1 collective-permute-start.2
  37.4 2.1 copy.51
  39.5 96.0 %collective-permute-done.3 = bf16[12,4,16,1536]{3,2,1,0:T(8,128)(2,1)} collective-permute-done((bf16[12,4,16,1536]{3,2,1,0:T(8,128)(2,1)}, bf16[12,4,16,1536]{3,2,1,0:T(8,128)(2,1)}, u32[]{:S(2)}, u32[]{:S(2)}) %collective-permute-start.3) | collective-permute-done | bytes 2359328 | tf_op jit(solution)/shard_map/ppermute | solution.py:18
  135.5 9.7 fusion.52
  145.2 213.1 %while.15 = (s32[]{:T(128)}, f32[12,256,128]{1,2,0:T(8,128)}, f32[12,12,12,16,128]{4,3,2,1,0:T(8,128)}, s32[12]{0:T(128)S(1)}, bf16[2,128,1536]{2,1,0:T(8,128)(2...) while((s32[]{:T(128)}, f32[12,256,128]{1,2,0:T(8,128)}, ...), condition=%wide.region_5.6_spmd, body=%wide.region_0.5_spmd.sunk | while | flops 499376128 | bytes 40042176 | solution.py:185
  254.1 2.0 dynamic-slice_bitcast_fusion.4
  358.3 9.7 convert.8
  368.0 6.3 fusion.75
  374.3 100.0 %collective-permute-start.5 = (bf16[12,12,4,16,128]{4,3,2,1,0:T(8,128)(2,1)}, bf16[12,12,4,16,128]{4,3,2,1,0:T(8,128)(2,1)}, u32[]{:S(2)}, u32[]{:S(2)}) collective-permute-start(bf16[12,12,4,16,128]{4,3,2,1,0:T(8,128)(2,1)} %get-tuple-element.230), channel_id=1, source_target_pairs={{0,1},{1,2},{2,3},{3,4},{4,5},{5,6},{6,7},{7,8},{8,9},{9,10},{10,1... | collective-permute-start | bytes 7077896 | tf_op jit(solution)/shard_map/ppermute | solution.py:26
  477.4 2.6 add_convert_fusion
  479.9 44.1 %collective-permute-done.5 = bf16[12,12,4,16,128]{4,3,2,1,0:T(8,128)(2,1)} collective-permute-done((bf16[12,12,4,16,128]{4,3,2,1,0:T(8,128)(2,1)}, bf16[12,12,4,16,128]{4,3,2,1,0:T(8,128)(2,1)}, u32[]{:S(2)}, u32[]{:S(2)}) %collective-permute-start.5) | collective-permute-done | bytes 2359328 | tf_op jit(solution)/shard_map/ppermute | solution.py:26
  524.0 103.1 %collective-permute-done.4 = bf16[12,12,4,16,128]{4,3,2,1,0:T(8,128)(2,1)} collective-permute-done((bf16[12,12,4,16,128]{4,3,2,1,0:T(8,128)(2,1)}, bf16[12,12,4,16,128]{4,3,2,1,0:T(8,128)(2,1)}, u32[]{:S(2)}, u32[]{:S(2)}) %collective-permute-start.4) | collective-permute-done | bytes 2359328 | tf_op jit(solution)/shard_map/ppermute | solution.py:26
  627.1 7.4 fusion.71
  638.1 3.8 collective-permute-start.6
  643.3 2.0 fusion.77
  651.5 2.2 fusion.54
  656.1 2.2 fusion.55
  659.0 3.7 fusion.56
  668.0 71.2 %all-reduce.6.cloned.1.call-done = f32[16384]{0:T(1024)} async-done(((f32[16384]{0:T(1024)}), f32[16384]{0:T(1024)}) %all-reduce.6.cloned.1.call-update) | async-done | bytes 65552 | tf_op jit(solution)/shard_map/psum | solution.py:229
  740.3 398.5 %all-reduce.8.cloned.1.call-done = f32[16384]{0:T(1024)} async-done(((f32[16384]{0:T(1024)}), f32[16384]{0:T(1024)}) %all-reduce.8.cloned.1.call-update) | async-done | bytes 65552 | tf_op jit(solution)/shard_map/psum | solution.py:229
  (339 shorter events, 207.2 us)
Async XLA Ops:
  7.2 469.7 %copy-start = (bf16[256,3072]{1,0:T(8,128)(2,1)S(1)}, bf16[256,3072]{1,0:T(8,128)(2,1)}, u32[]{:S(2)}) copy-start(bf16[256,3072]{1,0:T(8,128)(2,1)} %param.18) | copy-start | bytes 4718596
  7.2 30.2 %copy-start.6 = (bf16[4,4,16,1536]{3,2,1,0:T(8,128)(2,1)S(1)}, bf16[4,4,16,1536]{3,2,1,0:T(8,128)(2,1)}, u32[]{:S(2)}) copy-start(bf16[4,4,16,1536]{3,2,1,0:T(8,128)(2,1)} %param.19) | copy-start | bytes 2359300
  7.2 732.1 %all-reduce.6.cloned.1.call-start = ((), (), s32[]{:S(2)}) async-start(), calls=%async_computation | async-start | bytes 131072 | tf_op jit(solution)/shard_map/psum | solution.py:229
  7.2 13.7 %collective-permute-start = (bf16[4,4,16,1536]{3,2,1,0:T(8,128)(2,1)}, bf16[4,4,16,1536]{3,2,1,0:T(8,128)(2,1)S(1)}, u32[]{:S(2)}, u32[]{:S(2)}) collective-permute-start(bf16[4,4,16,1536]{3,2,1,0:T(8,128)(2,1)} %param.20), channel_id=1, source_target_pairs={{0,32},{32,64},{64,96},{96,128},{128,160},{160,192},{192,224},{1,3... | collective-permute-start | bytes 2359304 | tf_op jit(solution)/shard_map/ppermute | solution.py:15
  9.3 14.7 %collective-permute-start.1 = (bf16[4,4,16,1536]{3,2,1,0:T(8,128)(2,1)}, bf16[4,4,16,1536]{3,2,1,0:T(8,128)(2,1)S(1)}, u32[]{:S(2)}, u32[]{:S(2)}) collective-permute-start(bf16[4,4,16,1536]{3,2,1,0:T(8,128)(2,1)} %param.20), channel_id=1, source_target_pairs={{32,0},{64,32},{96,64},{128,96},{160,128},{192,160},{224,192},{33,... | collective-permute-start | bytes 2359304 | tf_op jit(solution)/shard_map/ppermute | solution.py:18
  24.9 110.5 %collective-permute-start.3 = (bf16[12,4,16,1536]{3,2,1,0:T(8,128)(2,1)}, bf16[12,4,16,1536]{3,2,1,0:T(8,128)(2,1)}, u32[]{:S(2)}, u32[]{:S(2)}) collective-permute-start(bf16[12,4,16,1536]{3,2,1,0:T(8,128)(2,1)} %constant_dynamic-update-slice_fusion), channel_id=1, source_target_pairs={{1,0},{2,1},{3,2},{4,3},{5,4},{6,5},{7,6},{8,7},{9,8},{10,9},{11,1... | collective-permute-start | bytes 7077896 | tf_op jit(solution)/shard_map/ppermute | solution.py:18
  26.2 109.2 %collective-permute-start.2 = (bf16[12,4,16,1536]{3,2,1,0:T(8,128)(2,1)}, bf16[12,4,16,1536]{3,2,1,0:T(8,128)(2,1)}, u32[]{:S(2)}, u32[]{:S(2)}) collective-permute-start(bf16[12,4,16,1536]{3,2,1,0:T(8,128)(2,1)} %constant_dynamic-update-slice_fusion), channel_id=1, source_target_pairs={{0,1},{1,2},{2,3},{3,4},{4,5},{5,6},{6,7},{7,8},{8,9},{9,10},{10,1... | collective-permute-start | bytes 7077896 | tf_op jit(solution)/shard_map/ppermute | solution.py:15
  39.5 105.7 %copy-start.9 = (s32[12,3]{0,1:T(4,128)S(1)}, s32[12,3]{0,1:T(4,128)}, u32[]{:S(2)}) copy-start(s32[12,3]{0,1:T(4,128)} %param.23) | copy-start | bytes 436
  162.9 4.4 copy-start.4
  180.7 4.5 copy-start.4
  251.7 4.5 copy-start.4
  304.9 4.4 copy-start.4
  322.7 4.4 copy-start.4
  340.5 4.4 copy-start.4
  368.0 108.9 %copy-start.8 = (bf16[3072,16]{0,1:T(8,128)(2,1)S(1)}, bf16[3072,16]{0,1:T(8,128)(2,1)}, u32[]{:S(2)}) copy-start(bf16[3072,16]{0,1:T(8,128)(2,1)} %param.28) | copy-start | bytes 294916
  374.3 149.7 %collective-permute-start.5 = (bf16[12,12,4,16,128]{4,3,2,1,0:T(8,128)(2,1)}, bf16[12,12,4,16,128]{4,3,2,1,0:T(8,128)(2,1)}, u32[]{:S(2)}, u32[]{:S(2)}) collective-permute-start(bf16[12,12,4,16,128]{4,3,2,1,0:T(8,128)(2,1)} %get-tuple-element.230), channel_id=1, source_target_pairs={{0,1},{1,2},{2,3},{3,4},{4,5},{5,6},{6,7},{7,8},{8,9},{9,10},{10,1... | collective-permute-start | bytes 7077896 | tf_op jit(solution)/shard_map/ppermute | solution.py:26
  474.2 152.9 %collective-permute-start.4 = (bf16[12,12,4,16,128]{4,3,2,1,0:T(8,128)(2,1)}, bf16[12,12,4,16,128]{4,3,2,1,0:T(8,128)(2,1)}, u32[]{:S(2)}, u32[]{:S(2)}) collective-permute-start(bf16[12,12,4,16,128]{4,3,2,1,0:T(8,128)(2,1)} %get-tuple-element.229), channel_id=1, source_target_pairs={{1,0},{2,1},{3,2},{4,3},{5,4},{6,5},{7,6},{8,7},{9,8},{10,9},{11,1... | collective-permute-start | bytes 7077896 | tf_op jit(solution)/shard_map/ppermute | solution.py:26
  634.5 7.3 copy-start.3
  634.5 8.8 copy-start.10
  636.1 13.6 %collective-permute-start.7 = (bf16[12,4,4,16,128]{4,3,2,1,0:T(8,128)(2,1)}, bf16[12,4,4,16,128]{4,3,2,1,0:T(8,128)(2,1)}, u32[]{:S(2)}, u32[]{:S(2)}) collective-permute-start(bf16[12,4,4,16,128]{4,3,2,1,0:T(8,128)(2,1)} %get-tuple-element.232), channel_id=1, source_target_pairs={{0,32},{32,64},{64,96},{96,128},{128,160},{160,192},{192,224},{1,3... | collective-permute-start | bytes 2359304 | tf_op jit(solution)/shard_map/ppermute | solution.py:26
  638.1 13.5 %collective-permute-start.6 = (bf16[12,4,4,16,128]{4,3,2,1,0:T(8,128)(2,1)}, bf16[12,4,4,16,128]{4,3,2,1,0:T(8,128)(2,1)}, u32[]{:S(2)}, u32[]{:S(2)}) collective-permute-start(bf16[12,4,4,16,128]{4,3,2,1,0:T(8,128)(2,1)} %get-tuple-element.231), channel_id=1, source_target_pairs={{32,0},{64,32},{96,64},{128,96},{160,128},{192,160},{224,192},{33,... | collective-permute-start | bytes 2359304 | tf_op jit(solution)/shard_map/ppermute | solution.py:26
  659.0 5.5 copy-start.7
  664.5 74.8 %copy-start.2 = (bf16[12,4,4,16,128]{4,3,2,1,0:T(8,128)(2,1)S(1)}, bf16[12,4,4,16,128]{4,3,2,1,0:T(8,128)(2,1)}, u32[]{:S(2)}) copy-start(bf16[12,4,4,16,128]{4,3,2,1,0:T(8,128)(2,1)} %copy-done.1) | copy-start | bytes 2359300
  668.0 470.8 %all-reduce.8.cloned.1.call-start = ((), (), s32[]{:S(2)}) async-start(), calls=%async_computation.1 | async-start | bytes 131072 | tf_op jit(solution)/shard_map/psum | solution.py:229
  (19 other events, 41.6 us)
Sparse Core Ops, SparseCore 0:
  668.1 71.1 all-reduce.5
  742.1 396.6 all-reduce.7
